TPU v7x, 512 devices: a whole 4x4x16 slice. The times are simulated.
512 devices in a mesh: blk: 128 (over y, z, core), ex: 4 (over x).
Axes of the slice: x: 4, y: 4, z: 16, core: 2. Of those that a mesh axis runs over, the one named last changes fastest.
Arguments:
- hidden: bfloat16 [16, 256, 11008], P('ex', None, 'blk'), may hold values from -6 to 6
- out_grad: bfloat16 [16, 256, 4096], P('ex', None, 'blk'), may hold values from -0.5625 to 0.5625
- example_len: int32 [16], P('ex'), may hold values from 1 to 256, 2048 in all
- sign_bits: int32 [16384, 4096], P('blk'), may hold values 0 or 1
- kept_rows: int32 [8192], replicated, may hold values from 0 to 16383
- kept_cols: int32 [8192], replicated, may hold values from 0 to 4095
Outputs:
- sketch: float32 [16, 8192], P(None, ('blk', 'ex'))
All inputs are finite; a program needn't handle non-finite values. No bound on the sum of `example_len` or of `sign_bits` on one device may be relied on, other than what follows from the above.
Results may differ from a plain program's by a relative error of at most 0.0003.
Values may be sent and summed in bfloat16 or wider, within the bound.
A program may use at most 64 MiB of HBM per device.

v0:
```python
import math

import jax
import jax.numpy as jnp
from jax import lax
from jax.sharding import PartitionSpec as P


def parity_sign(first_bits, second_bits):
    folded = jnp.bitwise_and(first_bits, second_bits)
    for shift_by in (16, 8, 4, 2, 1):
        folded = jnp.bitwise_xor(folded, jnp.right_shift(folded, shift_by))
    return (1 - 2 * jnp.bitwise_and(folded, 1)).astype(jnp.float32)


def sylvester(order):
    positions_all = lax.iota(jnp.int32, order)
    return parity_sign(positions_all[:, None], positions_all[None, :])


def hadamard_cols(values, width):
    top_precision = lax.Precision.HIGHEST
    low_width = min(width, 128)
    high_width = width // low_width
    lead = values.shape[0]
    middle = values.shape[1]
    shaped = values.reshape(lead, middle, high_width, low_width)
    shaped = jnp.einsum("ab,epbc->epac", sylvester(high_width), shaped, precision=top_precision)
    shaped = jnp.einsum("epac,fc->epaf", shaped, sylvester(low_width), precision=top_precision)
    return shaped.reshape(lead, middle, width)


def local(hidden, out_grad, example_len, sign_bits, kept_rows, kept_cols):
    num_examples = hidden.shape[0]
    seq_len = hidden.shape[1]
    rows_blk = hidden.shape[2]
    pad_rows = sign_bits.shape[0]
    col_width = sign_bits.shape[1]
    blk_count = lax.axis_size("blk")
    blk_index = lax.axis_index("blk")
    total_len = pad_rows * blk_count * col_width
    top_precision = lax.Precision.HIGHEST
    positions = lax.iota(jnp.int32, seq_len)
    token_mask = (positions[None, :] < example_len[:, None]).astype(jnp.bfloat16)
    masked = hidden * token_mask[:, :, None]
    h_rows = sylvester(pad_rows)[:, :rows_blk]
    kept_block = kept_rows // pad_rows
    kept_pos = kept_rows % pad_rows
    sign_rows = (1 - 2 * sign_bits[:rows_blk]).astype(jnp.float32)
    columns = lax.all_gather(out_grad, "blk", axis=2, tiled=True)
    gradient = jnp.einsum("etr,etd->erd", masked, columns, preferred_element_type=jnp.float32)
    weighted = gradient * sign_rows[None]
    mixed_vals = jnp.einsum("pr,erd->epd", h_rows, weighted, precision=top_precision)
    mixed_vals = hadamard_cols(mixed_vals, col_width)
    flat_index = kept_pos * col_width + kept_cols
    picked = jnp.take(mixed_vals.reshape(num_examples, pad_rows * col_width), flat_index, axis=1)
    picked = picked * parity_sign(kept_block, blk_index)[None, :]
    summed = lax.psum_scatter(picked, "blk", scatter_dimension=1, tiled=True)
    result = lax.all_to_all(summed, "ex", split_axis=1, concat_axis=0, tiled=True)
    return result / math.sqrt(total_len)


def solution(mesh):
    return jax.shard_map(
        local,
        mesh=mesh,
        in_specs=(P("ex", None, "blk"), P("ex", None, "blk"), P("ex"), P("blk", None), P(), P()),
        out_specs=P(None, ("blk", "ex")),
        check_vma=False,
    )
```

profile of v0, /device:TPU:2, one launch (start us, length us, event | category | flops | bytes accessed | tf_op | source)
XLA Modules:
  0.0 605.1 jit_solution(930672221179984338)
XLA Ops:
  6.5 0.0 all-gather.2.cloned.1.call-start
  6.5 0.7 all-gather.2.cloned.1.call-update
  7.3 0.0 reduce-scatter.4.cloned.1.call-start
  7.4 0.7 fusion.32
  8.1 0.8 compare_and_fusion
  8.9 0.8 subtract_convert_fusion.1
  9.7 0.9 broadcast_multiply_fusion
  10.7 1.5 subtract_convert_fusion
  12.2 149.8 %all-gather.2.cloned.1.call-done = bf16[4,256,4096]{1,2,0:T(8,128)(2,1)} async-done(((bf16[4,256,32]{1,2,0:T(8,128)(2,1)}), bf16[4,256,4096]{1,2,0:T(8,128)(2,1)}) %all-gather.2.cloned.1.call-update) | async-done | bytes 8388624 | tf_op jit(solution)/shard_map/all_gather | solution.py:50
  162.0 6.1 %convolution_multiply_fusion = f32[4,86,4096]{2,1,0:T(8,128)S(1)} fusion(bf16[4,256,4096]{1,2,0:T(8,128)(2,1)} %all-gather.2.cloned.1.call-done, f32[86,4096]{1,0:T(8,128)S(1)} %subtract_convert_fusion, bf16[4,256,86]{1,0,2:T(4,128)(2,1)S(1)} %bitcast.41), kind=kOutput, calls=%fused_computation.4 | convolution fusion | flops 722829312 | bytes 15609856 | tf_op jit(solution)/shard_map/etr,etd->erd/dot_general | solution.py:51
  168.1 15.7 %fusion.8 = f32[4,4096,128]{2,1,0:T(8,128)} fusion(f32[4,86,4096]{2,1,0:T(8,128)S(1)} %convolution_multiply_fusion, f32[128,128]{0,1:T(8,128)S(1)} %fusion.6), kind=kOutput, calls=%fused_computation.31 | convolution fusion | flops 2164260864 | bytes 14200832 | tf_op jit(solution)/shard_map/pr,erd->epd/dot_general | solution.py:53
  183.8 10.3 %copy.13 = f32[4,128,32,128]{3,2,1,0:T(8,128)} copy(f32[4,128,32,128]{1,3,2,0:T(8,128)} %bitcast.38) | data formatting | bytes 16777216 | tf_op jit(solution)/shard_map/reshape | solution.py:27
  194.0 10.1 %fusion.22 = f32[4,128,128,32]{2,3,1,0:T(8,128)S(1)} fusion(f32[4,128,32,128]{3,2,1,0:T(8,128)} %copy.13), kind=kOutput, calls=%fused_computation.52 | convolution fusion | flops 805321728 | bytes 16777216 | tf_op jit(solution)/shard_map/ab,epbc->epac/dot_general | solution.py:28
  204.1 10.5 %fusion = f32[4,128,32,128]{3,2,1,0:T(8,128)S(1)} fusion(f32[4,128,128,32]{2,3,1,0:T(8,128)S(1)} %fusion.22), kind=kOutput, calls=%fused_computation.2 | convolution fusion | flops 3221471232 | bytes 16777216 | tf_op jit(solution)/shard_map/epac,fc->epaf/dot_general | solution.py:29
  214.6 18.7 %copy.31 = f32[1,4,4096,128]{3,1,2,0:T(4,128)} copy(f32[1,4,4096,128]{3,2,1,0:T(8,128)S(1)} %bitcast.39) | data formatting | bytes 16777216
  233.2 92.5 %gather_fusion = f32[8192,4]{0,1:T(4,128)S(1)} fusion(f32[4,524288]{1,0:T(4,128)} %bitcast.37, s32[8192]{0:T(1024)S(1)} %broadcast_clamp_fusion), kind=kCustom, calls=%fused_computation | custom fusion | bytes 294912 | tf_op jit(solution)/shard_map/jit(_take)/gather | solution.py:56
  325.8 0.1 multiply_bitcast_fusion
  325.9 2.6 copy.23
  328.5 0.0 reduce-scatter.4.cloned.1.call-update
  328.5 259.8 %reduce-scatter.4.cloned.1.call-done = f32[64,4]{1,0:T(8,128)} async-done(((f32[8192,4]{1,0:T(8,128)}), f32[64,4]{1,0:T(8,128)}) %reduce-scatter.4.cloned.1.call-update) | async-done | bytes 1040
  588.3 0.9 copy.17
  589.1 8.5 %all_to_all.13 = f32[4,4,16]{2,0,1:T(4,128)S(1)} all-to-all(f32[4,4,16]{2,0,1:T(4,128)S(1)} %copy.17), channel_id=1, replica_groups=mesh['blk'=128,'ex'=4] {'ex'}, dimensions={1} | all-to-all | bytes 2048 | tf_op jit(solution)/shard_map/all_to_all | solution.py:59
  597.6 0.6 broadcast_multiply_fusion.1
  (3 shorter events, 0.1 us)
Async XLA Ops:
  6.5 155.5 %all-gather.2.cloned.1.call-start = ((), (), s32[]{:S(2)}) async-start(), calls=%async_computation.2 | async-start | bytes 8454144 | tf_op jit(solution)/shard_map/all_gather | solution.py:50
  7.3 581.0 %reduce-scatter.4.cloned.1.call-start = ((), (), s32[]{:S(2)}) async-start(), calls=%async_computation.3 | async-start | bytes 4227072
Sparse Core Ops, SparseCore 0:
  10.5 151.4 all-gather.1
  328.6 259.6 reduce-scatter.3
where the time goes:
time: 608 us; the launch traced here: 605 us
  waiting for transfers between devices  410 us (67%)
  local copies, waits for them, and re-layouts  125 us (21%)
  matrix products  42.3 us (7%)
  between operations  13.5 us (2%)
  blocking collectives  8.48 us (1%)
    unnamed x3, waiting for transfers between devices  260 us
    all_gather x1, waiting for transfers between devices, local(): columns = lax.all_gather(out_grad, 'blk', axis=2, tiled=True)  150 us
    gather x1, local copies, waits for them, and re-layouts, local(): jnp.take(mixed_vals.reshape(num_examples, pad_rows * col_width), flat_ind...  92.5 us
    unnamed x3, local copies, waits for them, and re-layouts  21.3 us
    dot_general x1, matrix products, local(): jnp.einsum('pr,erd->epd', h_rows, weighted, precision=top_precision)  15.7 us
  transfers between devices with their start and end apart: 2, of which 2 were waited for; matrix products, arithmetic and copies ran while one was open for 1% of the time, Pallas kernels for 0%

commit v1 on v0

v1 whole, which is shorter than its diff:
```python
import functools
import math

import jax
import jax.numpy as jnp
from jax import lax
from jax.experimental import pallas as pl
from jax.experimental.pallas import tpu as pltpu
from jax.sharding import PartitionSpec as P

NY, NZ, NC, NX = 4, 16, 2, 4
NE = 4
TOK = 256
JW = 32
RP = 96
NK = 11
NG = 4
GW = 256
VMEM_MB = 56 << 20
NT = (((1,), (1,)), ((), ()))
TN = (((0,), (0,)), ((), ()))


def parity(bits):
    for shift_by in (16, 8, 4, 2, 1):
        bits = jnp.bitwise_xor(bits, jnp.right_shift(bits, shift_by))
    return jnp.bitwise_and(bits, 1)


def sylvester_tile(rows, cols, row_mask, col_mask):
    a = jnp.bitwise_and(lax.broadcasted_iota(jnp.int32, (rows, cols), 0), row_mask)
    b = jnp.bitwise_and(lax.broadcasted_iota(jnp.int32, (rows, cols), 1), col_mask)
    return (1 - 2 * parity(jnp.bitwise_and(a, b))).astype(jnp.float32)


def split(values):
    hi = values.astype(jnp.bfloat16)
    lo = (values - hi.astype(jnp.float32)).astype(jnp.bfloat16)
    return hi, lo


def device(y, z, c, x):
    return ((y * NZ + z) * NC + c, x)


def place():
    b = lax.axis_index("blk")
    return b // (NZ * NC), (b // NC) % NZ, b % NC, lax.axis_index("ex")


def butterfly(values, width):
    values = list(values) + [None] * (width - len(values))
    step = width // 2
    while step:
        for base in range(0, width, 2 * step):
            for j in range(base, base + step):
                a, b = values[j], values[j + step]
                values[j], values[j + step] = (a, a) if b is None else (a + b, a - b)
        step //= 2
    return values


LINES = 4
CH = LINES * 128
GROUP = 32
KHI = 16


def spread_rows(xs, flat, g):
    def mix(rb, carry):
        rows = pl.ds(pl.multiple_of(rb * 8, 8), 8)
        for p, v in enumerate(butterfly([xs[k, rows, :] for k in range(NK)], KHI)):
            flat[pl.ds(pl.multiple_of((p * NG + g) * GW + rb * 8, 8), 8), :] = v
        return carry

    lax.fori_loop(0, GW // 8, mix, 0)


def join_groups(flat):
    def mix(rb, carry):
        for p in range(KHI):
            rows = [pl.ds(pl.multiple_of((p * NG + g) * GW + rb * 8, 8), 8) for g in range(NG)]
            for g, v in enumerate(butterfly([flat[r, :] for r in rows], NG)):
                flat[rows[g], :] = v
        return carry

    lax.fori_loop(0, GW // 8, mix, 0)


def make_picker(kr_ref, kc_ref, idx_smem, table_ref, out_ref, y, zc, scale):
    row = lax.broadcasted_iota(jnp.int32, (128, 128), 0)
    lane = lax.broadcasted_iota(jnp.int32, (128, 128), 1)
    owner = jnp.bitwise_and((lane >> 5) + y, NY - 1)
    code = row & 31
    bits = jnp.bitwise_or(jnp.bitwise_and(code >> 3, owner) << 3, jnp.bitwise_and(code, lane) & 7)
    hx = (1 - 2 * parity(bits)).astype(jnp.float32)
    hx = jnp.where((row >> 5) == ((lane >> 3) & (NE - 1)), hx, 0.0).astype(jnp.bfloat16)
    weights = jnp.concatenate([hx, hx], axis=1)
    which = lax.broadcasted_iota(jnp.int32, (32, 128), 0)

    def pick(ch, rows_ref):
        for h in range(LINES):
            line = ch * LINES + h
            for g in range(128 // GROUP):
                rows = [table_ref[pl.ds(idx_smem[line, g * GROUP + u], 1), :] for u in range(GROUP)]
                for u in range(GROUP):
                    rows_ref[pl.ds(h * 128 + g * GROUP + u, 1), :] = rows[u]

    def finish(ch, rows_ref):
        parts = []
        for h in range(LINES):
            line = ch * LINES + h
            kr = kr_ref[pl.ds(line, 1), :]
            kc = kc_ref[pl.ds(line, 1), :]
            flips = jnp.bitwise_xor(jnp.bitwise_and((kr >> 7) & 31, zc), jnp.bitwise_and(kc >> 10, y) << 5)
            sign = (1 - 2 * parity(flips)).astype(jnp.float32) * scale
            parts.append(jnp.where(which == ((kr >> 12) << 3) + jnp.bitwise_and(kr, 7), sign, 0.0))
        onehot = jnp.concatenate(parts, axis=1)
        hi, lo = split(rows_ref[...])
        both = jnp.concatenate([hi, lo], axis=1)
        prod = lax.dot_general(weights, both, NT, preferred_element_type=jnp.float32)
        for e in range(NE):
            res = jnp.sum(prod[32 * e:32 * e + 32] * onehot, axis=0, keepdims=True)
            for h in range(LINES):
                out_ref[ch * LINES + h, pl.ds(e, 1), :] = res[:, 128 * h:128 * h + 128]

    return pick, finish


def remote(src, dst, send, recv, target):
    return pltpu.make_async_remote_copy(
        src_ref=src, dst_ref=dst, send_sem=send, recv_sem=recv,
        device_id=target, device_id_type=pl.DeviceIdType.MESH)


def landed(ref, sem):
    pltpu.make_async_copy(ref, ref, sem).wait()


def greet(peers):
    barrier = pltpu.get_barrier_semaphore()
    for peer in peers:
        pl.semaphore_signal(barrier, inc=1, device_id=peer, device_id_type=pl.DeviceIdType.MESH)
    return barrier


def sketch_kernel(own_ref, h_ref, len_ref, sb_ref, krh_ref, kch_ref, out_ref,
                  cols, kr_ref, kc_ref, hin, mall, sall, sout, hbuf, sown, sfor, wbuf, xs, table, rows_a, rows_b, idx_ref, idx_smem,
                  pbuf, ybuf, zsum, zbuf, tbuf, xbuf,
                  r_send, r_recv, p_recv, m_send, m_recv, s_send, s_recv, x_send, x_recv,
                  c_send, c_recv, load_sem, idx_sem, sb_sem, ysend, yrecv, zsend, zrecv, xsend, xrecv, *, scale):
    y, z, c, x = place()
    zpeers = (device(y, (z + 1) % NZ, c, x), device(y, (z + NZ - 1) % NZ, c, x))
    sibling = device(y, z, 1 - c, x)
    ypeers = [device((y + k) % NY, z, c, x) for k in range(1, NY)]
    xpeers = (device(y, z, c, (x + 1) % NX), device(y, z, c, (x + NX - 1) % NX))
    zall = [device(y, (z + k) % NZ, c, x) for k in range(1, NZ)]
    offsets = [(dc, dx) for dx in range(NX) for dc in range(NC) if dc or dx]
    square = [device(y, z, (c + dc) % NC, (x + dx) % NX) for dc, dx in offsets]
    cross = (device(y, (z + 1) % NZ, 1 - c, x), device(y, (z + NZ - 1) % NZ, 1 - c, x))
    peers = list(zpeers) + list(cross) + ypeers + square + zall[1:-1]
    barrier = greet(peers)

    def sign_rows(k):
        width = GW if k else NG * GW
        start = ((y + k) % NY) * (NG * GW) + (x * GW if k else 0)
        src = sb_ref.at[pl.ds(0, RP), pl.ds(pl.multiple_of(start, GW), width)]
        return pltpu.make_async_copy(src, sfor.at[k - 1] if k else sown, sb_sem.at[k])

    loads = [pltpu.make_async_copy(src, dst, load_sem.at[i]) for i, (src, dst) in enumerate((
        (own_ref, cols.at[z, c]), (h_ref, hin), (krh_ref, kr_ref), (kch_ref, kc_ref)))]
    loads[0].start()
    for k in (1, 2, 3):
        sign_rows(k).start()
    for load in loads[1:]:
        load.start()
    sign_rows(0).start()

    def slab(sign, s):
        return (z + NZ - s) % NZ if sign == 0 else (z + s) % NZ

    def ring(sign, half, s, arrival=False):
        part = cols.at[slab(sign, s), c, pl.ds(2 * half, 2)]
        first = isinstance(s, int) and s == 0 and not arrival
        return remote(own_ref.at[pl.ds(2 * half, 2)] if first else part, part, r_send,
                      r_recv.at[sign, half, s if arrival else s + 1], zpeers[sign])

    def last_ring(sign, arrival=False):
        part = cols.at[slab(sign, 8 if arrival else 7), 1 - c if arrival else c, pl.ds(2 * sign, 2)]
        return remote(part, part, c_send, c_recv, cross[sign])

    def pair(sign, s, arrival=False):
        part = cols.at[slab(sign, s), 1 - c if arrival else c]
        return remote(part, part, r_send, p_recv.at[0 if s < 4 else (1 if s < 6 else 2)], sibling)

    def m_copy(side, part, arrival=False):
        there = 3 if side == 0 else 1
        piece = pl.ds(2 * part, 2)
        dst = mall.at[there, piece]
        return remote(dst if arrival else mall.at[0, piece], dst, m_send, m_recv.at[side, 0 if part == side else 1],
                      ypeers[0] if side == 0 else ypeers[2])

    def m_relay(side, arrival=False):
        part = pl.ds(2 * side, 2)
        dst = mall.at[2, part]
        src = mall.at[3 if side == 0 else 1, part]
        return remote(dst if arrival else src, dst, m_send, m_recv.at[2, side],
                      ypeers[0] if side == 0 else ypeers[2])

    def s_copy(k, arrival=False):
        dst = sall.at[NY - k, x]
        return remote(dst if arrival else sout.at[k - 1], dst, s_send, s_recv, ypeers[k - 1])

    def x_copy(side, arrival=False):
        group = x if not arrival else ((x + NX - 1) % NX if side == 0 else (x + 1) % NX)
        part = sall.at[pl.ds(1, NY - 1), group]
        return remote(part, part, x_send, x_recv.at[side], xpeers[side])

    def x_relay(side, arrival=False):
        if arrival:
            group = (x + 2) % NX
        else:
            group = (x + NX - 1) % NX if side == 0 else (x + 1) % NX
        part = sall.at[pl.ds(1, NY - 1), group, pl.ds(side * (RP // 2), RP // 2)]
        return remote(part, part, x_send, x_recv.at[2], xpeers[side])

    def signs(bits):
        return (1 - 2 * bits).astype(jnp.float32).astype(jnp.bfloat16)

    pl.semaphore_wait(barrier, len(peers))
    for half in range(2):
        for sign in range(2):
            ring(sign, half, 0).start()
    loads[0].wait()
    pair(0, 0).start()
    for k in range(1, NY):
        sign_rows(k).wait()
        sout[k - 1] = signs(sfor[k - 1])
        s_copy(k).start()
    loads[1].wait()
    rows_blk = h_ref.shape[0]
    hbuf[0:rows_blk] = hin[...].astype(jnp.float32)
    hbuf[rows_blk:RP] = jnp.zeros((RP - rows_blk, NE, TOK), jnp.float32)
    lane = lax.broadcasted_iota(jnp.int32, (RP, TOK), 1)
    for e in range(NE):
        mall[0, e] = jnp.where(lane < len_ref[e], hbuf[:, e, :], 0.0).astype(jnp.bfloat16)
    for side in range(2):
        m_copy(side, side).start()
    for side in range(2):
        m_copy(side, 1 - side).start()
    loads[2].wait()
    loads[3].wait()
    kpos = jnp.bitwise_and(kr_ref[...], 127)
    idx_ref[...] = (kpos >> 3) * (NG * GW) + jnp.bitwise_and(kc_ref[...], NG * GW - 1)
    to_smem = pltpu.make_async_copy(idx_ref, idx_smem, idx_sem)
    to_smem.start()
    sign_rows(0).wait()
    for g in range(NG):
        sall[0, g] = signs(sown[:, GW * g:GW * g + GW])
    h256 = sylvester_tile(GW, GW, 255, 255).astype(jnp.bfloat16)

    def step(s):
        for half in range(2):
            for sign in range(2):
                ring(sign, half, s, True).wait_recv()
                if s < 7 or half == sign:
                    ring(sign, half, s).start()
                if s == 7 and half == sign:
                    last_ring(sign).start()
        for sign in range(2):
            pair(sign, s).start()

    def compute(g):
        for e in range(NE):
            lhs = mall[:, e].reshape(NY * RP, TOK)
            rhs = cols[pl.ds(NG * g, NG), :, e].reshape(GW, TOK)
            grad = lax.dot_general(lhs, rhs, NT, preferred_element_type=jnp.float32)
            for b in range(NY):
                w = grad[RP * b:RP * b + RP] * sall[b, g].astype(jnp.float32)
                for k in range(NK):
                    wbuf[k, 32 * b + 8 * e:32 * b + 8 * e + 8] = w[8 * k:8 * k + 8]
        for k in range(0, NK, 2):
            n = min(2, NK - k)
            hi, lo = split(wbuf[k:k + n].reshape(128 * n, GW))
            out = (lax.dot_general(h256, hi, NT, preferred_element_type=jnp.float32)
                   + lax.dot_general(h256, lo, NT, preferred_element_type=jnp.float32))
            for i in range(n):
                xs[k + i] = out[:, 128 * i:128 * i + 128]

    step(1)
    step(2)
    landed(sout, s_recv)
    for side in range(2):
        x_copy(side).start()
    step(3)
    step(4)
    for side in range(2):
        m_copy(side, side, True).wait_recv()
        m_relay(side).start()
    for side in range(2):
        x_copy(side, True).wait_recv()
        x_relay(side).start()
    flat = table
    mine = z // NG
    low = z % NG < 2
    early = jnp.where(low, (mine + NG - 1) % NG, (mine + 1) % NG)
    late = jnp.where(low, (mine + 1) % NG, (mine + NG - 1) % NG)

    def stage(t, carry):
        @pl.when(t == 0)
        def _():
            step(5)
            step(6)
            landed(cols.at[pl.ds(0, 7), 0], p_recv.at[0])
            for side in range(2):
                m_copy(side, 1 - side, True).wait_recv()
                m_relay(side, True).wait_recv()
            landed(sall.at[pl.ds(1, NY - 1), 0], x_recv.at[2])

        @pl.when(t == 1)
        def _():
            step(7)
            landed(cols.at[pl.ds(0, 4), 0], p_recv.at[1])

        @pl.when(t == 2)
        def _():
            landed(cols.at[pl.ds(0, 4), 0], p_recv.at[2])

        @pl.when(t == 3)
        def _():
            for sign in range(2):
                ring(sign, sign, 8, True).wait_recv()
            landed(cols.at[0, 0], c_recv)

        g = jnp.where(t == 0, mine, jnp.where(t == 1, early, jnp.where(t == 2, late, (mine + 2) % NG)))
        compute(g)
        spread_rows(xs, flat, g)
        return carry

    lax.fori_loop(0, NG, stage, 0)
    join_groups(flat)
    to_smem.wait()
    pick, finish = make_picker(kr_ref, kc_ref, idx_smem, table, pbuf, y, z * NC + c, scale)
    quarter = pbuf.shape[0] // NY
    per = quarter // LINES

    def y_copy(k):
        far = (y + k) % NY
        return remote(pbuf.at[pl.ds(far * quarter, quarter)], ybuf.at[k - 1], ysend, yrecv,
                      device(far, z, c, x))

    def turn(q):
        return jnp.where(q == 0, 2, jnp.where(q == 1, 1, 3))

    def chunk_at(j):
        other = ((y + turn(j // per)) % NY) * per + j % per
        off = jnp.where(j == 12, 2, jnp.where(j == 13, 1, jnp.where(j == 14, 3, 0)))
        return jnp.where(j < 12, other, y * per + (z // LINES + off) % per)

    def z_copy(k):
        far = (z + k) % NZ
        return remote(zsum.at[far], zbuf.at[k - 1], zsend, zrecv, device(y, far, c, x))

    def add_up(far):
        total = pbuf[y * quarter + far]
        for k in range(1, NY):
            total = total + ybuf[k - 1, far]
        zsum[far] = total

    def emit(j, own):
        first = LINES * (chunk_at(j) - y * per)
        for h in range(LINES):
            far = first + h
            add_up(far)
            if own:
                @pl.when(far != z)
                def _():
                    z_copy((far + NZ - z) % NZ).start()
            else:
                z_copy((far + NZ - z) % NZ).start()

    def drain():
        landed(cols.at[pl.ds(0, NZ - 1)], r_send)
        landed(cols.at[0, 0], c_send)
        landed(mall.at[pl.ds(0, NY - 1)], m_send)
        landed(sout, s_send)
        landed(sall.at[pl.ds(0, 3), pl.ds(0, 3)], x_send)

    pick(chunk_at(0), rows_a)

    def body(n, carry):
        pick(chunk_at(2 * n + 1), rows_b)
        finish(chunk_at(2 * n), rows_a)
        pick(chunk_at(2 * n + 2), rows_a)
        finish(chunk_at(2 * n + 1), rows_b)

        @pl.when((n < 6) & (n % 2 == 1))
        def _():
            y_copy(turn(n // 2)).start()

        @pl.when(n == 6)
        def _():
            landed(ybuf, yrecv)
            emit(12, False)
            emit(13, False)

        return carry

    lax.fori_loop(0, 7, body, 0)
    pick(chunk_at(15), rows_b)
    finish(chunk_at(14), rows_a)
    emit(14, False)
    finish(chunk_at(15), rows_b)
    emit(15, True)
    drain()
    landed(zbuf, zrecv)
    total = zsum[z]
    for k in range(1, NZ):
        total = total + zbuf[k - 1]
    tbuf[...] = total

    def last_copy(i):
        return remote(tbuf, xbuf.at[i], xsend, xrecv, square[i])

    for i in range(len(offsets)):
        last_copy(i).start()
    landed(ybuf, ysend)
    landed(zbuf, zsend)
    landed(xbuf, xrecv)
    slot = {o: i for i, o in enumerate(offsets)}
    for dx in range(NX):
        first = total if dx == 0 else xbuf[slot[(0, dx)]]
        out_ref[(x - dx + NX) % NX] = first + xbuf[slot[(1, dx)]]

    landed(xbuf, xsend)


def local(hidden, out_grad, example_len, sign_bits, kept_rows, kept_cols):
    keep = kept_rows.shape[0]
    total_len = sign_bits.shape[0] * lax.axis_size("blk") * sign_bits.shape[1]
    blk_index = lax.axis_index("blk")
    dma = pltpu.SemaphoreType.DMA
    vm = pl.BlockSpec(memory_space=pltpu.VMEM)
    hbm = pl.BlockSpec(memory_space=pl.ANY)

    f32 = jnp.float32
    blocks = pl.pallas_call(
        functools.partial(sketch_kernel, scale=1.0 / math.sqrt(total_len)),
        out_shape=jax.ShapeDtypeStruct((NX, NE, 128), f32),
        in_specs=[hbm, hbm, pl.BlockSpec(memory_space=pltpu.SMEM), hbm, hbm, hbm],
        out_specs=vm,
        scratch_shapes=[
            pltpu.VMEM((NZ, NC, NE, JW, TOK), jnp.bfloat16),
            pltpu.VMEM((keep // 128, 128), jnp.int32), pltpu.VMEM((keep // 128, 128), jnp.int32),
            pltpu.VMEM((hidden.shape[2], NE, TOK), jnp.bfloat16),
            pltpu.VMEM((NY, NE, RP, TOK), jnp.bfloat16),
            pltpu.VMEM((NY, NG, RP, GW), jnp.bfloat16),
            pltpu.VMEM((NY - 1, RP, GW), jnp.bfloat16),
            pltpu.VMEM((RP, NE, TOK), f32),
            pltpu.VMEM((RP, NG * GW), jnp.int32),
            pltpu.VMEM((NY - 1, RP, GW), jnp.int32),
            pltpu.VMEM((NK, 128, GW), f32),
            pltpu.VMEM((NK, GW, 128), f32),
            pltpu.VMEM((KHI * NG * GW, 128), f32),
            pltpu.VMEM((CH, 128), f32), pltpu.VMEM((CH, 128), f32),
            pltpu.VMEM((keep // 128, 128), jnp.int32), pltpu.SMEM((keep // 128, 128), jnp.int32),
            pltpu.VMEM((keep // 128, NE, 128), f32),
            pltpu.VMEM((NY - 1, NZ, NE, 128), f32),
            pltpu.VMEM((NZ, NE, 128), f32),
            pltpu.VMEM((NZ - 1, NE, 128), f32),
            pltpu.VMEM((NE, 128), f32),
            pltpu.VMEM((7, NE, 128), f32),
            dma, dma((2, 2, 9)), dma((3,)), dma, dma((3, 2)),
            dma, dma, dma, dma((3,)),
            dma, dma, dma((4,)), dma, dma((NY,)), dma, dma, dma, dma, dma, dma,
        ],
        compiler_params=pltpu.CompilerParams(
            collective_id=0, has_side_effects=True, vmem_limit_bytes=VMEM_MB),
    )(out_grad.transpose(0, 2, 1), hidden.transpose(2, 0, 1), example_len, sign_bits,
      kept_rows.reshape(keep // 128, 128), kept_cols.reshape(keep // 128, 128))
    start = (blk_index % NC) * 64 + lax.axis_index("ex") * 16
    return lax.dynamic_slice_in_dim(blocks.reshape(4 * NE, 128), start, 16, axis=1)


def solution(mesh):
    return jax.shard_map(
        local,
        mesh=mesh,
        in_specs=(P("ex", None, "blk"), P("ex", None, "blk"), P("ex"), P("blk", None), P(), P()),
        out_specs=P(None, ("blk", "ex")),
        check_vma=False,
    )
```

time: 608 us -> 72.1 us (0.12)
  the two profiles are of different devices: /device:TPU:2 before, /device:TPU:1 now
where the time goes in v1:
time: 72.1 us; the launch traced here: 71.9 us
  Pallas kernels  70.5 us (98%)
  local copies, waits for them, and re-layouts  1.37 us (2%)
    pallas_call x1, Pallas kernels, local(): pl.pallas_call(functools.partial(sketch_kernel, scale=1.0 / math.sqrt(tot...  70.5 us

profile of v1, /device:TPU:1, one launch (start us, length us, event | category | flops | bytes accessed | tf_op | source)
XLA Modules:
  0.0 71.9 jit_solution(11264919788091257468)
XLA Ops:
  0.0 70.5 %shard_map.64 = f32[4,4,128]{2,1,0:T(4,128)} custom-call(bf16[4,32,256]{2,1,0:T(8,128)(2,1)} %bitcast.6, bf16[86,4,256]{2,1,0:T(4,128)(2,1)} %bitcast.5, s32[4]{0:T(128)} %len_ref.1, s32[128,4096]{1,0:T(8,128)} %sb_ref.1, s32[64,128]{1,0:T(8,128)} %bitcast.7, s32[64,128]{1,0:T(8,128)} %bitcast.8), custom_call_target="tpu_custom_call" | custom-call | tf_op jit(solution)/shard_map/pallas_call | solution.py:447
  70.5 1.4 %constant_dynamic-slice_fusion = f32[16,16]{1,0:T(8,128)} fusion(f32[16,128]{1,0:T(8,128)} %bitcast.9, s32[]{:T(128)S(6)} %select_n.11), kind=kLoop, calls=%fused_computation | loop fusion | bytes 2052 | tf_op jit(solution)/shard_map/dynamic_slice | solution.py:482

commit v2 on v1

--- a/solution.py
+++ b/solution.py
@@ -73,7 +73,7 @@
             flat[pl.ds(pl.multiple_of((p * NG + g) * GW + rb * 8, 8), 8), :] = v
         return carry
 
-    lax.fori_loop(0, GW // 8, mix, 0)
+    lax.fori_loop(0, GW // 8, mix, 0, unroll=4)
 
 
 def join_groups(flat):
@@ -84,7 +84,7 @@
                 flat[rows[g], :] = v
         return carry
 
-    lax.fori_loop(0, GW // 8, mix, 0)
+    lax.fori_loop(0, GW // 8, mix, 0, unroll=2)
 
 
 def make_picker(kr_ref, kc_ref, idx_smem, table_ref, out_ref, y, zc, scale):
@@ -180,9 +180,9 @@
         return (z + NZ - s) % NZ if sign == 0 else (z + s) % NZ
 
     def ring(sign, half, s, arrival=False):
-        part = cols.at[slab(sign, s), c, pl.ds(2 * half, 2)]
+        part = cols.at[slab(sign, s), c, half]
         first = isinstance(s, int) and s == 0 and not arrival
-        return remote(own_ref.at[pl.ds(2 * half, 2)] if first else part, part, r_send,
+        return remote(own_ref.at[half] if first else part, part, r_send,
                       r_recv.at[sign, half, s if arrival else s + 1], zpeers[sign])
 
     def last_ring(sign, arrival=False):
@@ -228,7 +228,7 @@
         return (1 - 2 * bits).astype(jnp.float32).astype(jnp.bfloat16)
 
     pl.semaphore_wait(barrier, len(peers))
-    for half in range(2):
+    for half in range(NE):
         for sign in range(2):
             ring(sign, half, 0).start()
     loads[0].wait()
@@ -260,13 +260,14 @@
     h256 = sylvester_tile(GW, GW, 255, 255).astype(jnp.bfloat16)
 
     def step(s):
-        for half in range(2):
+        for half in range(NE):
             for sign in range(2):
                 ring(sign, half, s, True).wait_recv()
-                if s < 7 or half == sign:
+                if s < 7 or half // 2 == sign:
                     ring(sign, half, s).start()
-                if s == 7 and half == sign:
-                    last_ring(sign).start()
+        if s == 7:
+            for sign in range(2):
+                last_ring(sign).start()
         for sign in range(2):
             pair(sign, s).start()
 
@@ -329,7 +330,8 @@
         @pl.when(t == 3)
         def _():
             for sign in range(2):
-                ring(sign, sign, 8, True).wait_recv()
+                for half in (2 * sign, 2 * sign + 1):
+                    ring(sign, half, 8, True).wait_recv()
             landed(cols.at[0, 0], c_recv)
 
         g = jnp.where(t == 0, mine, jnp.where(t == 1, early, jnp.where(t == 2, late, (mine + 2) % NG)))
@@ -470,7 +472,7 @@
             pltpu.VMEM((NZ - 1, NE, 128), f32),
             pltpu.VMEM((NE, 128), f32),
             pltpu.VMEM((7, NE, 128), f32),
-            dma, dma((2, 2, 9)), dma((3,)), dma, dma((3, 2)),
+            dma, dma((2, NE, 9)), dma((3,)), dma, dma((3, 2)),
             dma, dma, dma, dma((3,)),
             dma, dma, dma((4,)), dma, dma((NY,)), dma, dma, dma, dma, dma, dma,
         ],

time: 72.1 us -> 71.3 us (0.989)
  Pallas kernels: 70.5 us -> 69.7 us
    pallas_call x1, Pallas kernels: 70.5 us -> 69.7 us  [local(): pl.pallas_call(functools.partial(sketch_kernel, scale=1.0 / math.sqrt(tot...]
where the time goes in v2:
time: 71.3 us; the launch traced here: 71.1 us
  Pallas kernels  69.7 us (98%)
  local copies, waits for them, and re-layouts  1.37 us (2%)
    pallas_call x1, Pallas kernels, local(): pl.pallas_call(functools.partial(sketch_kernel, scale=1.0 / math.sqrt(tot...  69.7 us

profile of v2, /device:TPU:1, one launch (start us, length us, event | category | flops | bytes accessed | tf_op | source)
XLA Modules:
  0.0 71.1 jit_solution(5507479717537649179)
XLA Ops:
  0.0 69.7 %shard_map.64 = f32[4,4,128]{2,1,0:T(4,128)} custom-call(bf16[4,32,256]{2,1,0:T(8,128)(2,1)} %bitcast.6, bf16[86,4,256]{2,1,0:T(4,128)(2,1)} %bitcast.5, s32[4]{0:T(128)} %len_ref.1, s32[128,4096]{1,0:T(8,128)} %sb_ref.1, s32[64,128]{1,0:T(8,128)} %bitcast.7, s32[64,128]{1,0:T(8,128)} %bitcast.8), custom_call_target="tpu_custom_call" | custom-call | tf_op jit(solution)/shard_map/pallas_call | solution.py:449
  69.7 1.4 %constant_dynamic-slice_fusion = f32[16,16]{1,0:T(8,128)} fusion(f32[16,128]{1,0:T(8,128)} %bitcast.9, s32[]{:T(128)S(6)} %select_n.11), kind=kLoop, calls=%fused_computation | loop fusion | bytes 2052 | tf_op jit(solution)/shard_map/dynamic_slice | solution.py:484

commit v3 on v2

--- a/solution.py
+++ b/solution.py
@@ -87,7 +87,7 @@
     lax.fori_loop(0, GW // 8, mix, 0, unroll=2)
 
 
-def make_picker(kr_ref, kc_ref, idx_smem, table_ref, out_ref, y, zc, scale):
+def make_picker(kr_ref, kc_ref, idx_smem, table_ref, out_ref, hot, wpick, y, zc, scale):
     row = lax.broadcasted_iota(jnp.int32, (128, 128), 0)
     lane = lax.broadcasted_iota(jnp.int32, (128, 128), 1)
     owner = jnp.bitwise_and((lane >> 5) + y, NY - 1)
@@ -95,8 +95,18 @@
     bits = jnp.bitwise_or(jnp.bitwise_and(code >> 3, owner) << 3, jnp.bitwise_and(code, lane) & 7)
     hx = (1 - 2 * parity(bits)).astype(jnp.float32)
     hx = jnp.where((row >> 5) == ((lane >> 3) & (NE - 1)), hx, 0.0).astype(jnp.bfloat16)
-    weights = jnp.concatenate([hx, hx], axis=1)
+    wpick[...] = jnp.concatenate([hx, hx], axis=1)
     which = lax.broadcasted_iota(jnp.int32, (32, 128), 0)
+
+    def prepare(line, carry):
+        kr = kr_ref[pl.ds(line, 1), :]
+        kc = kc_ref[pl.ds(line, 1), :]
+        flips = jnp.bitwise_xor(jnp.bitwise_and((kr >> 7) & 31, zc), jnp.bitwise_and(kc >> 10, y) << 5)
+        sign = (1 - 2 * parity(flips)).astype(jnp.float32) * scale
+        hot[line] = jnp.where(which == ((kr >> 12) << 3) + jnp.bitwise_and(kr, 7), sign, 0.0)
+        return carry
+
+    lax.fori_loop(0, kr_ref.shape[0], prepare, 0, unroll=4)
 
     def pick(ch, rows_ref):
         for h in range(LINES):
@@ -107,18 +117,10 @@
                     rows_ref[pl.ds(h * 128 + g * GROUP + u, 1), :] = rows[u]
 
     def finish(ch, rows_ref):
-        parts = []
-        for h in range(LINES):
-            line = ch * LINES + h
-            kr = kr_ref[pl.ds(line, 1), :]
-            kc = kc_ref[pl.ds(line, 1), :]
-            flips = jnp.bitwise_xor(jnp.bitwise_and((kr >> 7) & 31, zc), jnp.bitwise_and(kc >> 10, y) << 5)
-            sign = (1 - 2 * parity(flips)).astype(jnp.float32) * scale
-            parts.append(jnp.where(which == ((kr >> 12) << 3) + jnp.bitwise_and(kr, 7), sign, 0.0))
-        onehot = jnp.concatenate(parts, axis=1)
+        onehot = jnp.concatenate([hot[ch * LINES + h] for h in range(LINES)], axis=1)
         hi, lo = split(rows_ref[...])
         both = jnp.concatenate([hi, lo], axis=1)
-        prod = lax.dot_general(weights, both, NT, preferred_element_type=jnp.float32)
+        prod = lax.dot_general(wpick[...], both, NT, preferred_element_type=jnp.float32)
         for e in range(NE):
             res = jnp.sum(prod[32 * e:32 * e + 32] * onehot, axis=0, keepdims=True)
             for h in range(LINES):
@@ -145,9 +147,9 @@
 
 
 def sketch_kernel(own_ref, h_ref, len_ref, sb_ref, krh_ref, kch_ref, out_ref,
-                  cols, kr_ref, kc_ref, hin, mall, sall, sout, hbuf, sown, sfor, wbuf, xs, table, rows_a, rows_b, idx_ref, idx_smem,
+                  cols, kr_ref, kc_ref, hin, mall, sall, sout, hbuf, sown, sfor, wbuf, xs, table, rows_a, rows_b, hot, wpick, idx_ref, idx_smem,
                   pbuf, ybuf, zsum, zbuf, tbuf, xbuf,
-                  r_send, r_recv, p_recv, m_send, m_recv, s_send, s_recv, x_send, x_recv,
+                  r_send, r_recv, p_recv, m_send, m_recv, s_send, s_recv, x_send, x_recv, xr_recv,
                   c_send, c_recv, load_sem, idx_sem, sb_sem, ysend, yrecv, zsend, zrecv, xsend, xrecv, *, scale):
     y, z, c, x = place()
     zpeers = (device(y, (z + 1) % NZ, c, x), device(y, (z + NZ - 1) % NZ, c, x))
@@ -209,20 +211,17 @@
 
     def s_copy(k, arrival=False):
         dst = sall.at[NY - k, x]
-        return remote(dst if arrival else sout.at[k - 1], dst, s_send, s_recv, ypeers[k - 1])
-
-    def x_copy(side, arrival=False):
+        return remote(dst if arrival else sout.at[k - 1], dst, s_send, s_recv.at[k - 1], ypeers[k - 1])
+
+    def x_copy(side, k, arrival=False):
         group = x if not arrival else ((x + NX - 1) % NX if side == 0 else (x + 1) % NX)
-        part = sall.at[pl.ds(1, NY - 1), group]
-        return remote(part, part, x_send, x_recv.at[side], xpeers[side])
-
-    def x_relay(side, arrival=False):
-        if arrival:
-            group = (x + 2) % NX
-        else:
-            group = (x + NX - 1) % NX if side == 0 else (x + 1) % NX
-        part = sall.at[pl.ds(1, NY - 1), group, pl.ds(side * (RP // 2), RP // 2)]
-        return remote(part, part, x_send, x_recv.at[2], xpeers[side])
+        part = sall.at[k, group]
+        return remote(part, part, x_send, x_recv.at[side, k - 1], xpeers[side])
+
+    def x_relay(side, k):
+        group = (x + NX - 1) % NX if side == 0 else (x + 1) % NX
+        part = sall.at[k, group, pl.ds(side * (RP // 2), RP // 2)]
+        return remote(part, part, x_send, xr_recv, xpeers[side])
 
     def signs(bits):
         return (1 - 2 * bits).astype(jnp.float32).astype(jnp.bfloat16)
@@ -272,12 +271,13 @@
             pair(sign, s).start()
 
     def compute(g):
+        turned = [sall[b, g].astype(jnp.float32) for b in range(NY)]
         for e in range(NE):
             lhs = mall[:, e].reshape(NY * RP, TOK)
             rhs = cols[pl.ds(NG * g, NG), :, e].reshape(GW, TOK)
             grad = lax.dot_general(lhs, rhs, NT, preferred_element_type=jnp.float32)
             for b in range(NY):
-                w = grad[RP * b:RP * b + RP] * sall[b, g].astype(jnp.float32)
+                w = grad[RP * b:RP * b + RP] * turned[b]
                 for k in range(NK):
                     wbuf[k, 32 * b + 8 * e:32 * b + 8 * e + 8] = w[8 * k:8 * k + 8]
         for k in range(0, NK, 2):
@@ -290,17 +290,20 @@
 
     step(1)
     step(2)
-    landed(sout, s_recv)
-    for side in range(2):
-        x_copy(side).start()
+    for k in (1, 3, 2):
+        s_copy(k, True).wait_recv()
+        for side in range(2):
+            x_copy(side, NY - k).start()
     step(3)
+    pick, finish = make_picker(kr_ref, kc_ref, idx_smem, table, pbuf, hot, wpick, y, z * NC + c, scale)
     step(4)
     for side in range(2):
         m_copy(side, side, True).wait_recv()
         m_relay(side).start()
-    for side in range(2):
-        x_copy(side, True).wait_recv()
-        x_relay(side).start()
+    for k in (3, 1, 2):
+        for side in range(2):
+            x_copy(side, k, True).wait_recv()
+            x_relay(side, k).start()
     flat = table
     mine = z // NG
     low = z % NG < 2
@@ -316,7 +319,7 @@
             for side in range(2):
                 m_copy(side, 1 - side, True).wait_recv()
                 m_relay(side, True).wait_recv()
-            landed(sall.at[pl.ds(1, NY - 1), 0], x_recv.at[2])
+            landed(sall.at[pl.ds(1, NY - 1), 0], xr_recv)
 
         @pl.when(t == 1)
         def _():
@@ -342,7 +345,6 @@
     lax.fori_loop(0, NG, stage, 0)
     join_groups(flat)
     to_smem.wait()
-    pick, finish = make_picker(kr_ref, kc_ref, idx_smem, table, pbuf, y, z * NC + c, scale)
     quarter = pbuf.shape[0] // NY
     per = quarter // LINES
 
@@ -400,18 +402,14 @@
         def _():
             y_copy(turn(n // 2)).start()
 
-        @pl.when(n == 6)
-        def _():
-            landed(ybuf, yrecv)
-            emit(12, False)
-            emit(13, False)
-
         return carry
 
     lax.fori_loop(0, 7, body, 0)
     pick(chunk_at(15), rows_b)
     finish(chunk_at(14), rows_a)
-    emit(14, False)
+    landed(ybuf, yrecv)
+    for j in (12, 13, 14):
+        emit(j, False)
     finish(chunk_at(15), rows_b)
     emit(15, True)
     drain()
@@ -465,6 +463,7 @@
             pltpu.VMEM((NK, GW, 128), f32),
             pltpu.VMEM((KHI * NG * GW, 128), f32),
             pltpu.VMEM((CH, 128), f32), pltpu.VMEM((CH, 128), f32),
+            pltpu.VMEM((keep // 128, 32, 128), f32), pltpu.VMEM((128, 256), jnp.bfloat16),
             pltpu.VMEM((keep // 128, 128), jnp.int32), pltpu.SMEM((keep // 128, 128), jnp.int32),
             pltpu.VMEM((keep // 128, NE, 128), f32),
             pltpu.VMEM((NY - 1, NZ, NE, 128), f32),
@@ -473,7 +472,7 @@
             pltpu.VMEM((NE, 128), f32),
             pltpu.VMEM((7, NE, 128), f32),
             dma, dma((2, NE, 9)), dma((3,)), dma, dma((3, 2)),
-            dma, dma, dma, dma((3,)),
+            dma, dma((NY - 1,)), dma, dma((2, NY - 1)), dma,
             dma, dma, dma((4,)), dma, dma((NY,)), dma, dma, dma, dma, dma, dma,
         ],
         compiler_params=pltpu.CompilerParams(

time: 71.3 us -> 71.1 us (level)
  no operation moved by 1% of the time
where the time goes in v3:
time: 71.1 us; the launch traced here: 71 us
  Pallas kernels  69.6 us (98%)
  local copies, waits for them, and re-layouts  1.37 us (2%)
    pallas_call x1, Pallas kernels, local(): pl.pallas_call(functools.partial(sketch_kernel, scale=1.0 / math.sqrt(tot...  69.6 us

profile of v3, /device:TPU:1, one launch (start us, length us, event | category | flops | bytes accessed | tf_op | source)
XLA Modules:
  0.0 71.0 jit_solution(8019464552611933322)
XLA Ops:
  0.0 69.6 %shard_map.64 = f32[4,4,128]{2,1,0:T(4,128)} custom-call(bf16[4,32,256]{2,1,0:T(8,128)(2,1)} %bitcast.6, bf16[86,4,256]{2,1,0:T(4,128)(2,1)} %bitcast.5, s32[4]{0:T(128)} %len_ref.1, s32[128,4096]{1,0:T(8,128)} %sb_ref.1, s32[64,128]{1,0:T(8,128)} %bitcast.7, s32[64,128]{1,0:T(8,128)} %bitcast.8), custom_call_target="tpu_custom_call" | custom-call | tf_op jit(solution)/shard_map/pallas_call | solution.py:447
  69.6 1.4 %constant_dynamic-slice_fusion = f32[16,16]{1,0:T(8,128)} fusion(f32[16,128]{1,0:T(8,128)} %bitcast.9, s32[]{:T(128)S(6)} %select_n.11), kind=kLoop, calls=%fused_computation | loop fusion | bytes 2052 | tf_op jit(solution)/shard_map/dynamic_slice | solution.py:483

commit v4 on v3

--- a/solution.py
+++ b/solution.py
@@ -148,7 +148,7 @@
 
 def sketch_kernel(own_ref, h_ref, len_ref, sb_ref, krh_ref, kch_ref, out_ref,
                   cols, kr_ref, kc_ref, hin, mall, sall, sout, hbuf, sown, sfor, wbuf, xs, table, rows_a, rows_b, hot, wpick, idx_ref, idx_smem,
-                  pbuf, ybuf, zsum, zbuf, tbuf, xbuf,
+                  pbuf, ybuf, zsum, zbuf, tbuf, xbuf, res,
                   r_send, r_recv, p_recv, m_send, m_recv, s_send, s_recv, x_send, x_recv, xr_recv,
                   c_send, c_recv, load_sem, idx_sem, sb_sem, ysend, yrecv, zsend, zrecv, xsend, xrecv, *, scale):
     y, z, c, x = place()
@@ -171,65 +171,65 @@
 
     loads = [pltpu.make_async_copy(src, dst, load_sem.at[i]) for i, (src, dst) in enumerate((
         (own_ref, cols.at[z, c]), (h_ref, hin), (krh_ref, kr_ref), (kch_ref, kc_ref)))]
+
+    def slab(sign, s):
+        return (z + NZ - s) % NZ if sign == 0 else (z + s) % NZ
+
+    def ring(sign, half, s, arrival=False):
+        part = cols.at[slab(sign, s), c, half]
+        first = isinstance(s, int) and s == 0 and not arrival
+        return remote(own_ref.at[half] if first else part, part, r_send,
+                      r_recv.at[sign, half, s if arrival else s + 1], zpeers[sign])
+
+    def last_ring(sign, arrival=False):
+        part = cols.at[slab(sign, 8 if arrival else 7), 1 - c if arrival else c, pl.ds(2 * sign, 2)]
+        return remote(part, part, c_send, c_recv, cross[sign])
+
+    def pair(sign, s, arrival=False):
+        part = cols.at[slab(sign, s), 1 - c if arrival else c]
+        return remote(part, part, r_send, p_recv.at[0 if s < 4 else (1 if s < 6 else 2)], sibling)
+
+    def m_copy(side, part, arrival=False):
+        there = 3 if side == 0 else 1
+        piece = pl.ds(2 * part, 2)
+        dst = mall.at[there, piece]
+        return remote(dst if arrival else mall.at[0, piece], dst, m_send, m_recv.at[side, 0 if part == side else 1],
+                      ypeers[0] if side == 0 else ypeers[2])
+
+    def m_relay(side, arrival=False):
+        part = pl.ds(2 * side, 2)
+        dst = mall.at[2, part]
+        src = mall.at[3 if side == 0 else 1, part]
+        return remote(dst if arrival else src, dst, m_send, m_recv.at[2, side],
+                      ypeers[0] if side == 0 else ypeers[2])
+
+    def s_copy(k, arrival=False):
+        dst = sall.at[NY - k, x]
+        return remote(dst if arrival else sout.at[k - 1], dst, s_send, s_recv.at[k - 1], ypeers[k - 1])
+
+    def x_copy(side, k, arrival=False):
+        group = x if not arrival else ((x + NX - 1) % NX if side == 0 else (x + 1) % NX)
+        part = sall.at[k, group]
+        return remote(part, part, x_send, x_recv.at[side, k - 1], xpeers[side])
+
+    def x_relay(side, k):
+        group = (x + NX - 1) % NX if side == 0 else (x + 1) % NX
+        part = sall.at[k, group, pl.ds(side * (RP // 2), RP // 2)]
+        return remote(part, part, x_send, xr_recv, xpeers[side])
+
+    def signs(bits):
+        return (1 - 2 * bits).astype(jnp.float32).astype(jnp.bfloat16)
+
+    pl.semaphore_wait(barrier, len(peers))
+    for half in range(NE):
+        for sign in range(2):
+            ring(sign, half, 0).start()
     loads[0].start()
     for k in (1, 2, 3):
         sign_rows(k).start()
     for load in loads[1:]:
         load.start()
     sign_rows(0).start()
-
-    def slab(sign, s):
-        return (z + NZ - s) % NZ if sign == 0 else (z + s) % NZ
-
-    def ring(sign, half, s, arrival=False):
-        part = cols.at[slab(sign, s), c, half]
-        first = isinstance(s, int) and s == 0 and not arrival
-        return remote(own_ref.at[half] if first else part, part, r_send,
-                      r_recv.at[sign, half, s if arrival else s + 1], zpeers[sign])
-
-    def last_ring(sign, arrival=False):
-        part = cols.at[slab(sign, 8 if arrival else 7), 1 - c if arrival else c, pl.ds(2 * sign, 2)]
-        return remote(part, part, c_send, c_recv, cross[sign])
-
-    def pair(sign, s, arrival=False):
-        part = cols.at[slab(sign, s), 1 - c if arrival else c]
-        return remote(part, part, r_send, p_recv.at[0 if s < 4 else (1 if s < 6 else 2)], sibling)
-
-    def m_copy(side, part, arrival=False):
-        there = 3 if side == 0 else 1
-        piece = pl.ds(2 * part, 2)
-        dst = mall.at[there, piece]
-        return remote(dst if arrival else mall.at[0, piece], dst, m_send, m_recv.at[side, 0 if part == side else 1],
-                      ypeers[0] if side == 0 else ypeers[2])
-
-    def m_relay(side, arrival=False):
-        part = pl.ds(2 * side, 2)
-        dst = mall.at[2, part]
-        src = mall.at[3 if side == 0 else 1, part]
-        return remote(dst if arrival else src, dst, m_send, m_recv.at[2, side],
-                      ypeers[0] if side == 0 else ypeers[2])
-
-    def s_copy(k, arrival=False):
-        dst = sall.at[NY - k, x]
-        return remote(dst if arrival else sout.at[k - 1], dst, s_send, s_recv.at[k - 1], ypeers[k - 1])
-
-    def x_copy(side, k, arrival=False):
-        group = x if not arrival else ((x + NX - 1) % NX if side == 0 else (x + 1) % NX)
-        part = sall.at[k, group]
-        return remote(part, part, x_send, x_recv.at[side, k - 1], xpeers[side])
-
-    def x_relay(side, k):
-        group = (x + NX - 1) % NX if side == 0 else (x + 1) % NX
-        part = sall.at[k, group, pl.ds(side * (RP // 2), RP // 2)]
-        return remote(part, part, x_send, xr_recv, xpeers[side])
-
-    def signs(bits):
-        return (1 - 2 * bits).astype(jnp.float32).astype(jnp.bfloat16)
-
-    pl.semaphore_wait(barrier, len(peers))
-    for half in range(NE):
-        for sign in range(2):
-            ring(sign, half, 0).start()
     loads[0].wait()
     pair(0, 0).start()
     for k in range(1, NY):
@@ -430,7 +430,13 @@
     slot = {o: i for i, o in enumerate(offsets)}
     for dx in range(NX):
         first = total if dx == 0 else xbuf[slot[(0, dx)]]
-        out_ref[(x - dx + NX) % NX] = first + xbuf[slot[(1, dx)]]
+        res[(x - dx + NX) % NX] = first + xbuf[slot[(1, dx)]]
+    rows = res[...].reshape(NX * NE, 128)
+    mine_now = c * NX + x
+    owned = rows[:, 0:16]
+    for i in range(1, NC * NX):
+        owned = jnp.where(mine_now == i, rows[:, 16 * i:16 * i + 16], owned)
+    out_ref[...] = owned
 
     landed(xbuf, xsend)
 
@@ -438,15 +444,14 @@
 def local(hidden, out_grad, example_len, sign_bits, kept_rows, kept_cols):
     keep = kept_rows.shape[0]
     total_len = sign_bits.shape[0] * lax.axis_size("blk") * sign_bits.shape[1]
-    blk_index = lax.axis_index("blk")
     dma = pltpu.SemaphoreType.DMA
     vm = pl.BlockSpec(memory_space=pltpu.VMEM)
     hbm = pl.BlockSpec(memory_space=pl.ANY)
 
     f32 = jnp.float32
-    blocks = pl.pallas_call(
+    return pl.pallas_call(
         functools.partial(sketch_kernel, scale=1.0 / math.sqrt(total_len)),
-        out_shape=jax.ShapeDtypeStruct((NX, NE, 128), f32),
+        out_shape=jax.ShapeDtypeStruct((NX * NE, 16), f32),
         in_specs=[hbm, hbm, pl.BlockSpec(memory_space=pltpu.SMEM), hbm, hbm, hbm],
         out_specs=vm,
         scratch_shapes=[
@@ -471,6 +476,7 @@
             pltpu.VMEM((NZ - 1, NE, 128), f32),
             pltpu.VMEM((NE, 128), f32),
             pltpu.VMEM((7, NE, 128), f32),
+            pltpu.VMEM((NX, NE, 128), f32),
             dma, dma((2, NE, 9)), dma((3,)), dma, dma((3, 2)),
             dma, dma((NY - 1,)), dma, dma((2, NY - 1)), dma,
             dma, dma, dma((4,)), dma, dma((NY,)), dma, dma, dma, dma, dma, dma,
@@ -479,8 +485,6 @@
             collective_id=0, has_side_effects=True, vmem_limit_bytes=VMEM_MB),
     )(out_grad.transpose(0, 2, 1), hidden.transpose(2, 0, 1), example_len, sign_bits,
       kept_rows.reshape(keep // 128, 128), kept_cols.reshape(keep // 128, 128))
-    start = (blk_index % NC) * 64 + lax.axis_index("ex") * 16
-    return lax.dynamic_slice_in_dim(blocks.reshape(4 * NE, 128), start, 16, axis=1)
 
 
 def solution(mesh):

time: 71.1 us -> 71.9 us (1.011)
  Pallas kernels: 69.6 us -> 70.4 us
    dynamic_slice x1 -> x0, local copies, waits for them, and re-layouts: 1.37 us -> none  [local(): lax.dynamic_slice_in_dim(blocks.reshape(4 * NE, 128), start, 16, axis=1)]
    unnamed x0 -> x1, local copies, waits for them, and re-layouts: none -> 1.3 us
    pallas_call x1, Pallas kernels: 69.6 us -> 70.4 us  [local(): pl.pallas_call(functools.partial(sketch_kernel, scale=1.0 / math.sqrt(tot...]
where the time goes in v4:
time: 71.9 us; the launch traced here: 71.7 us
  Pallas kernels  70.4 us (98%)
  local copies, waits for them, and re-layouts  1.3 us (2%)
    pallas_call x1, Pallas kernels, local(): pl.pallas_call(functools.partial(sketch_kernel, scale=1.0 / math.sqrt(tot...  70.4 us

profile of v4, /device:TPU:1, one launch (start us, length us, event | category | flops | bytes accessed | tf_op | source)
XLA Modules:
  0.0 71.7 jit_solution(5078234339646464227)
XLA Ops:
  0.0 70.4 %shard_map.64 = f32[16,16]{1,0:T(8,128)} custom-call(bf16[4,32,256]{2,1,0:T(8,128)(2,1)} %bitcast.5, bf16[86,4,256]{2,1,0:T(4,128)(2,1)} %bitcast.4, s32[4]{0:T(128)} %len_ref.1, s32[128,4096]{1,0:T(8,128)} %sb_ref.1, s32[64,128]{1,0:T(8,128)} %bitcast.6, s32[64,128]{1,0:T(8,128)} %bitcast.7), custom_call_target="tpu_custom_call" | custom-call | tf_op jit(solution)/shard_map/pallas_call | solution.py:452
  70.4 1.3 %copy.8 = f32[16,16]{1,0:T(8,128)} copy(f32[16,16]{1,0:T(8,128)} %shard_map.64) | data formatting | bytes 2048
